TPU v7x, 128 devices: a whole 4x4x4 slice. The times are simulated.
128 devices in a mesh: ex: 16 (over y_hi, z, core), ey: 8 (over y_lo, x).
Axes of the slice: x: 4, y: 4 (y_hi: 2, y_lo: 2; y = y_hi * 2 + y_lo), z: 4, core: 2. Of those that a mesh axis runs over, the one named last changes fastest.
Arguments:
- tokens: bfloat16 [32768, 1536], P(('ex', 'ey')), may hold values from -6 to 6
- upstream: bfloat16 [32768, 1536], P(('ex', 'ey')), may hold values from -6 to 6
- route_one: int32 [32768, 1], P(('ex', 'ey')), may hold values from 0 to 15; in each aligned block of 256 rows (0 to 255, 256 to 511, ...) at most 32 rows name the same one
- route_two: int32 [32768, 1], P(('ex', 'ey')), may hold values from 0 to 63; in each aligned block of 256 rows (0 to 255, 256 to 511, ...) at most 8 rows name the same one
- keep_one: int32 [32768], P(('ex', 'ey')), may hold values 0 or 1
- keep_two: int32 [32768], P(('ex', 'ey')), may hold values 0 or 1
- gate_one: float32 [32768, 1], P(('ex', 'ey')), may hold values from 0.25 to 1
- gate_two: float32 [32768, 1], P(('ex', 'ey')), may hold values from 0.25 to 1
- up_one: bfloat16 [16, 1536, 1536], P('ex'), may hold values from -0.15625 to 0.15625
- down_one: bfloat16 [16, 1536, 1536], P('ex'), may hold values from -0.15625 to 0.15625
- up_two: bfloat16 [128, 1536, 768], P(('ex', 'ey')), may hold values from -0.15625 to 0.15625
- down_two: bfloat16 [128, 768, 1536], P(('ex', 'ey')), may hold values from -0.15625 to 0.15625
Outputs:
- result: bfloat16 [32768, 1536], P(('ex', 'ey'))
- grad_tokens: bfloat16 [32768, 1536], P(('ex', 'ey'))
- grad_up_one: bfloat16 [16, 1536, 1536], P('ex', 'ey')
- grad_down_one: bfloat16 [16, 1536, 1536], P('ex', 'ey')
- grad_up_two: bfloat16 [128, 1536, 768], P(('ex', 'ey'))
- grad_down_two: bfloat16 [128, 768, 1536], P(('ex', 'ey'))
Inputs may be any that keep to these rules, and one draw needn't show every extreme that they name: `route_one`: in every aligned block of 256 tokens no expert is named more than 32 times, a bound that some block reaches. `route_two`: in every aligned block of 256 tokens no expert is named more than 8 times, a bound that some block reaches.
All inputs are finite; a program needn't handle non-finite values. No bound on the sum of `keep_one` or of `keep_two` on one device may be relied on, other than what follows from the above.
Results may differ from a plain program's by a relative error of at most 0.02.
Values may be sent and summed in bfloat16 or wider, within the bound.
No kernel may reach another device: no remote copies, remote signals or barrier semaphores. Data moves between devices by JAX's collectives and lax.ppermute only.
A program may use at most 128 MiB of HBM per device.

v0:
```python
import jax
import jax.numpy as jnp
from jax import lax
from jax.sharding import PartitionSpec as P

EPS = 1e-06


def rms_scale(values):
    widened = values.astype(jnp.float32)
    return lax.rsqrt(jnp.mean(widened * widened, axis=-1, keepdims=True) + EPS)


def rms_normed(values):
    return (values.astype(jnp.float32) * rms_scale(values)).astype(jnp.bfloat16)


def rms_back(values, incoming):
    inv_rms = rms_scale(values)
    normed = values.astype(jnp.float32) * inv_rms
    grad_in = incoming.astype(jnp.float32)
    return inv_rms * (grad_in - normed * jnp.mean(grad_in * normed, axis=-1, keepdims=True))


def silu_slope(preact):
    sigmoid_value = jax.nn.sigmoid(preact)
    return sigmoid_value * (1.0 + preact * (1.0 - sigmoid_value))


def product(left_side, right_side):
    return jnp.dot(left_side, right_side, preferred_element_type=jnp.float32)


def product_back(left_side, right_side):
    return lax.dot_general(
        left_side, right_side, (((1,), (1,)), ((), ())), preferred_element_type=jnp.float32
    )


def product_rows(left_side, right_side):
    return lax.dot_general(
        left_side, right_side, (((0,), (0,)), ((), ())), preferred_element_type=jnp.float32
    )


def place_rows(route, keep, experts, capacity):
    chosen = route[:, 0]
    onehot = (chosen[:, None] == jnp.arange(experts, dtype=jnp.int32)[None, :]).astype(jnp.int32)
    before = jnp.cumsum(onehot, axis=0) - onehot
    slot_rank = jnp.sum(before * onehot, axis=1)
    return jnp.where(keep > 0, chosen * capacity + slot_rank, experts * capacity)


def fill_slots(values, target, experts, capacity):
    filled = (
        jnp.zeros((experts * capacity, values.shape[1]), values.dtype)
        .at[target]
        .set(values, mode="drop")
    )
    return filled.reshape(experts, capacity, values.shape[1])


def read_slots(filled, target):
    return jnp.take(filled.reshape(-1, filled.shape[-1]), target, axis=0, mode="fill", fill_value=0)


def first_send(filled):
    return lax.all_to_all(filled, "ex", split_axis=0, concat_axis=0, tiled=True)


def first_return(filled):
    return lax.all_to_all(filled, "ex", split_axis=0, concat_axis=0, tiled=True)


def wide_route(buffer):
    return lax.all_to_all(buffer, ("ex", "ey"), split_axis=0, concat_axis=0, tiled=True)


def second_send(filled):
    experts, capacity, model_width = filled.shape
    doubled = jnp.broadcast_to(filled[:, None], (experts, 2, capacity, model_width))
    return wide_route(doubled.reshape(2 * experts, capacity, model_width))


def second_return(partials):
    devices, capacity, model_width = partials.shape
    returned = wide_route(partials).reshape(devices // 2, 2, capacity, model_width)
    return (returned[:, 0].astype(jnp.float32) + returned[:, 1].astype(jnp.float32)).astype(
        jnp.bfloat16
    )


def per_device(
    tokens,
    upstream,
    route_one,
    route_two,
    keep_one,
    keep_two,
    gate_one,
    gate_two,
    up_one,
    down_one,
    up_two,
    down_two,
):
    count_x = lax.axis_size("ex")
    count_y = lax.axis_size("ey")
    devices = count_x * count_y
    tok_count = tokens.shape[0]
    model_width = tokens.shape[1]
    second_experts = devices // 2
    first_cap = 2 * tok_count // count_x
    second_cap = 2 * tok_count // second_experts
    target_one = place_rows(route_one, keep_one, count_x, first_cap)
    target_two = place_rows(route_two, keep_two, second_experts, second_cap)
    arrived_one = first_send(fill_slots(rms_normed(tokens), target_one, count_x, first_cap))
    rows_one = arrived_one.reshape(-1, model_width)
    pre_one = product(rows_one, up_one[0])
    hidden_one = jax.nn.silu(pre_one).astype(jnp.bfloat16)
    out_one = product(hidden_one, down_one[0]).astype(jnp.bfloat16).reshape(arrived_one.shape)
    collected_one = read_slots(first_return(out_one), target_one)
    middle = (tokens.astype(jnp.float32) + gate_one * collected_one.astype(jnp.float32)).astype(
        jnp.bfloat16
    )
    arrived_two = second_send(
        fill_slots(rms_normed(middle), target_two, second_experts, second_cap)
    )
    rows_two = arrived_two.reshape(-1, model_width)
    pre_two = product(rows_two, up_two[0])
    hidden_two = jax.nn.silu(pre_two).astype(jnp.bfloat16)
    part_two = product(hidden_two, down_two[0]).astype(jnp.bfloat16).reshape(arrived_two.shape)
    collected_two = read_slots(second_return(part_two), target_two)
    result = (middle.astype(jnp.float32) + gate_two * collected_two.astype(jnp.float32)).astype(
        jnp.bfloat16
    )
    send_two = (gate_two * upstream.astype(jnp.float32)).astype(jnp.bfloat16)
    grads_two = second_send(fill_slots(send_two, target_two, second_experts, second_cap)).reshape(
        -1, model_width
    )
    inner_two = (product_back(grads_two, down_two[0]) * silu_slope(pre_two)).astype(jnp.bfloat16)
    back_part = product_back(inner_two, up_two[0]).astype(jnp.bfloat16).reshape(arrived_two.shape)
    grad_up_two = product_rows(rows_two, inner_two).astype(jnp.bfloat16)[None]
    grad_down_two = product_rows(hidden_two, grads_two).astype(jnp.bfloat16)[None]
    back_two = read_slots(second_return(back_part), target_two)
    grad_middle = (upstream.astype(jnp.float32) + rms_back(middle, back_two)).astype(jnp.bfloat16)
    send_one = (gate_one * grad_middle.astype(jnp.float32)).astype(jnp.bfloat16)
    grads_one = first_send(fill_slots(send_one, target_one, count_x, first_cap)).reshape(
        -1, model_width
    )
    inner_one = (product_back(grads_one, down_one[0]) * silu_slope(pre_one)).astype(jnp.bfloat16)
    back_local = product_back(inner_one, up_one[0]).astype(jnp.bfloat16).reshape(arrived_one.shape)
    term_up = product_rows(rows_one, inner_one)
    term_down = product_rows(hidden_one, grads_one)
    share_up, share_down = (
        lax.psum_scatter(
            term_up.astype(jnp.bfloat16), "ey", scatter_dimension=0, tiled=True
        ).astype(jnp.float32),
        lax.psum_scatter(
            term_down.astype(jnp.bfloat16), "ey", scatter_dimension=0, tiled=True
        ).astype(jnp.float32),
    )
    back_one = read_slots(first_return(back_local), target_one)
    grad_tokens = (grad_middle.astype(jnp.float32) + rms_back(tokens, back_one)).astype(
        jnp.bfloat16
    )
    return (
        result,
        grad_tokens,
        share_up.astype(jnp.bfloat16)[None],
        share_down.astype(jnp.bfloat16)[None],
        grad_up_two,
        grad_down_two,
    )


def solution(mesh):
    return jax.shard_map(
        per_device,
        mesh=mesh,
        in_specs=(
            P(("ex", "ey"), None),
            P(("ex", "ey"), None),
            P(("ex", "ey"), None),
            P(("ex", "ey"), None),
            P(("ex", "ey")),
            P(("ex", "ey")),
            P(("ex", "ey"), None),
            P(("ex", "ey"), None),
            P("ex", None, None),
            P("ex", None, None),
            P(("ex", "ey"), None, None),
            P(("ex", "ey"), None, None),
        ),
        out_specs=(
            P(("ex", "ey"), None),
            P(("ex", "ey"), None),
            P("ex", "ey", None),
            P("ex", "ey", None),
            P(("ex", "ey"), None, None),
            P(("ex", "ey"), None, None),
        ),
        check_vma=False,
    )
```

profile of v0, /device:TPU:1, one launch (start us, length us, event | category | flops | bytes accessed | tf_op | source)
XLA Modules:
  0.0 466.5 jit_solution(15031823182230202357)
XLA Ops:
  7.2 1.5 fusion.56
  11.7 3.8 scatter_custom_fusion
  15.5 32.2 %all_to_all.40 = bf16[16,32,1536]{2,1,0:T(8,128)(2,1)S(1)} all-to-all(bf16[16,32,1536]{2,1,0:T(8,128)(2,1)} %bitcast.150), channel_id=1, replica_groups=mesh['ex'=16,'ey'=8] {'ex'}, dimensions={0} | all-to-all | bytes 3145728 | tf_op jit(solution)/shard_map/all_to_all | solution.py:68
  47.7 1.1 copy-done.12
  48.9 4.5 fusion.6
  53.4 3.8 fusion.28
  57.2 5.4 %all-to-all-start.1 = ((bf16[16,32,1536]{2,1,0:T(8,128)(2,1)}), bf16[16,32,1536]{2,1,0:T(8,128)(2,1)}, u32[]{:S(2)}, u32[]{:S(2)}) async-start(bf16[16,32,1536]{2,1,0:T(8,128)(2,1)} %bitcast.155), calls=%async_computation.1 | async-start | bytes 3145728 | tf_op jit(solution)/shard_map/all_to_all | solution.py:72
  63.7 22.0 %all-to-all-done.1 = bf16[16,32,1536]{2,1,0:T(8,128)(2,1)} async-done(((bf16[16,32,1536]{2,1,0:T(8,128)(2,1)}), bf16[16,32,1536]{2,1,0:T(8,128)(2,1)}, u32[]{:S(2)}, u32[]{:S(2)}) %all-to-all-start.1) | async-done | bytes 1572896 | tf_op jit(solution)/shard_map/all_to_all | solution.py:72
  85.7 4.6 gather_fusion
  90.3 2.5 fusion.58
  92.7 3.8 scatter_custom_fusion.1
  96.5 3.3 broadcast_in_dim.60
  99.9 7.9 %all-to-all-start.2 = ((bf16[128,8,1536]{2,1,0:T(8,128)(2,1)}), bf16[128,8,1536]{2,1,0:T(8,128)(2,1)}, u32[]{:S(2)}, u32[]{:S(2)}) async-start(bf16[128,8,1536]{2,1,0:T(8,128)(2,1)} %bitcast.148), calls=%async_computation.2 | async-start | bytes 6291456 | tf_op jit(solution)/shard_map/all_to_all | solution.py:76
  107.8 3.2 scatter_custom_fusion.2
  111.0 36.8 %all-to-all-done.2 = bf16[128,8,1536]{2,1,0:T(8,128)(2,1)} async-done(((bf16[128,8,1536]{2,1,0:T(8,128)(2,1)}), bf16[128,8,1536]{2,1,0:T(8,128)(2,1)}, u32[]{:S(2)}, u32[]{:S(2)}) %all-to-all-start.2) | async-done | bytes 3145760 | tf_op jit(solution)/shard_map/all_to_all | solution.py:76
  147.7 3.3 broadcast_in_dim.62
  151.0 5.8 %all-to-all-start.4 = ((bf16[128,8,1536]{2,1,0:T(8,128)(2,1)}), bf16[128,8,1536]{2,1,0:T(8,128)(2,1)}, u32[]{:S(2)}, u32[]{:S(2)}) async-start(bf16[128,8,1536]{2,1,0:T(8,128)(2,1)} %bitcast.147), calls=%async_computation.4 | async-start | bytes 6291456 | tf_op jit(solution)/shard_map/all_to_all | solution.py:76
  156.9 5.2 %fusion.17 = f32[1024,768]{1,0:T(8,128)S(1)} fusion(bf16[128,8,1536]{2,1,0:T(8,128)(2,1)} %all-to-all-done.2, bf16[1,1536,768]{2,1,0:T(8,128)(2,1)} %param.24), kind=kOutput, calls=%fused_computation.29 | convolution fusion | flops 2415919104 | bytes 8650752 | tf_op jit(solution)/shard_map/dot_general | solution.py:31
  162.1 1.6 copy-done.21
  163.7 4.0 fusion.11
  167.7 29.3 %all-to-all-done.4 = bf16[128,8,1536]{2,1,0:T(8,128)(2,1)} async-done(((bf16[128,8,1536]{2,1,0:T(8,128)(2,1)}), bf16[128,8,1536]{2,1,0:T(8,128)(2,1)}, u32[]{:S(2)}, u32[]{:S(2)}) %all-to-all-start.4) | async-done | bytes 3145760 | tf_op jit(solution)/shard_map/all_to_all | solution.py:76
  197.0 5.9 %all-to-all-start.3 = ((bf16[128,8,1536]{2,1,0:T(8,128)(2,1)}), bf16[128,8,1536]{2,1,0:T(8,128)(2,1)}, u32[]{:S(2)}, u32[]{:S(2)}) async-start(bf16[128,8,1536]{2,1,0:T(8,128)(2,1)} %fusion.11), calls=%async_computation.3 | async-start | bytes 6291456 | tf_op jit(solution)/shard_map/all_to_all | solution.py:76
  203.0 6.0 %multiply_convert_fusion = bf16[1024,768]{1,0:T(8,128)(2,1)S(1)} fusion(f32[1024,768]{1,0:T(8,128)} %copy-done.21, bf16[1,768,1536]{2,1,0:T(8,128)(2,1)S(1)} %copy-done, bf16[128,8,1536]{2,1,0:T(8,128)(2,1)} %all-to-all-done.4), kind=kOutput, calls=%fused_computation.32 | convolution fusion | flops 2422996992 | bytes 10223616 | tf_op jit(solution)/shard_map/dot_general | solution.py:35
  209.0 1.2 copy-done.27
  210.2 4.1 fusion.12
  214.3 28.9 %all-to-all-done.3 = bf16[128,8,1536]{2,1,0:T(8,128)(2,1)} async-done(((bf16[128,8,1536]{2,1,0:T(8,128)(2,1)}), bf16[128,8,1536]{2,1,0:T(8,128)(2,1)}, u32[]{:S(2)}, u32[]{:S(2)}) %all-to-all-start.3) | async-done | bytes 3145760 | tf_op jit(solution)/shard_map/all_to_all | solution.py:76
  243.2 5.9 %all-to-all-start.5 = ((bf16[128,8,1536]{2,1,0:T(8,128)(2,1)}), bf16[128,8,1536]{2,1,0:T(8,128)(2,1)}, u32[]{:S(2)}, u32[]{:S(2)}) async-start(bf16[128,8,1536]{2,1,0:T(8,128)(2,1)} %fusion.12), calls=%async_computation.5 | async-start | bytes 6291456 | tf_op jit(solution)/shard_map/all_to_all | solution.py:76
  249.4 2.3 fusion.60
  251.6 37.7 %all-to-all-done.5 = bf16[128,8,1536]{2,1,0:T(8,128)(2,1)} async-done(((bf16[128,8,1536]{2,1,0:T(8,128)(2,1)}), bf16[128,8,1536]{2,1,0:T(8,128)(2,1)}, u32[]{:S(2)}, u32[]{:S(2)}) %all-to-all-start.5) | async-done | bytes 3145760 | tf_op jit(solution)/shard_map/all_to_all | solution.py:76
  289.3 2.3 fusion.61
  291.5 2.1 gather_fusion.1
  293.7 1.3 gather_fusion.2
  296.6 2.8 fusion.49
  299.5 2.4 scatter_custom_fusion.3
  301.9 27.9 %all_to_all.41 = bf16[16,32,1536]{2,1,0:T(8,128)(2,1)S(1)} all-to-all(bf16[16,32,1536]{2,1,0:T(8,128)(2,1)S(1)} %bitcast.149), channel_id=1, replica_groups=mesh['ex'=16,'ey'=8] {'ex'}, dimensions={0} | all-to-all | bytes 3145728 | tf_op jit(solution)/shard_map/all_to_all | solution.py:68
  329.8 1.1 copy-done.14
  330.9 4.3 convolution_convert_fusion
  335.3 1.3 copy-done.15
  336.6 5.8 %fusion.31 = bf16[512,1536]{1,0:T(8,128)(2,1)S(1)} fusion(f32[512,1536]{1,0:T(8,128)} %copy-done.23, bf16[512,1536]{1,0:T(8,128)(2,1)S(1)} %bitcast.157, bf16[1,1536,1536]{2,1,0:T(8,128)(2,1)} %param.23), kind=kOutput, calls=%fused_computation.42 | convolution fusion | flops 2422996992 | bytes 11010048 | tf_op jit(solution)/shard_map/dot_general | solution.py:35
  343.6 4.4 convolution_convert_fusion.1
  348.0 1.4 copy-done.26
  349.4 6.1 %fusion.25 = bf16[512,1536]{1,0:T(8,128)(2,1)} fusion(bf16[512,1536]{1,0:T(8,128)(2,1)S(1)} %copy-done.26, bf16[1,1536,1536]{2,1,0:T(8,128)(2,1)} %param.22), kind=kOutput, calls=%fused_computation.40 | convolution fusion | flops 2416705536 | bytes 7864320 | tf_op jit(solution)/shard_map/dot_general | solution.py:35
  355.6 5.1 %all-to-all-start.7 = ((bf16[16,32,1536]{2,1,0:T(8,128)(2,1)}), bf16[16,32,1536]{2,1,0:T(8,128)(2,1)S(1)}, u32[]{:S(2)}, u32[]{:S(2)}) async-start(bf16[16,32,1536]{2,1,0:T(8,128)(2,1)} %bitcast.30), calls=%async_computation.7 | async-start | bytes 3145728 | tf_op jit(solution)/shard_map/all_to_all | solution.py:72
  360.7 6.1 %fusion.19 = bf16[1,1536,768]{2,1,0:T(8,128)(2,1)} fusion(bf16[1024,768]{1,0:T(8,128)(2,1)S(1)} %copy-done.28, bf16[128,8,1536]{2,1,0:T(8,128)(2,1)} %all-to-all-done.2), kind=kOutput, calls=%fused_computation.38 | convolution fusion | flops 2417098752 | bytes 7077888 | tf_op jit(solution)/shard_map/dot_general | solution.py:41
  366.9 5.9 %fusion.22 = bf16[1,768,1536]{2,1,0:T(8,128)(2,1)} fusion(bf16[128,8,1536]{2,1,0:T(8,128)(2,1)} %all-to-all-done.4, f32[1024,768]{1,0:T(8,128)S(1)} %copy-done.22), kind=kOutput, calls=%fused_computation.39 | convolution fusion | flops 2421030912 | bytes 8650752 | tf_op jit(solution)/shard_map/dot_general | solution.py:41
  372.7 80.6 %all-to-all-done.7 = bf16[16,32,1536]{2,1,0:T(8,128)(2,1)S(1)} async-done(((bf16[16,32,1536]{2,1,0:T(8,128)(2,1)}), bf16[16,32,1536]{2,1,0:T(8,128)(2,1)S(1)}, u32[]{:S(2)}, u32[]{:S(2)}) %all-to-all-start.7) | async-done | bytes 1572896 | tf_op jit(solution)/shard_map/all_to_all | solution.py:72
  453.3 1.3 gather_fusion.3
  456.6 2.6 fusion.52
  (85 shorter events, 9.1 us)
Async XLA Ops:
  7.2 156.6 %copy-start = (bf16[1,768,1536]{2,1,0:T(8,128)(2,1)S(1)}, bf16[1,768,1536]{2,1,0:T(8,128)(2,1)}, u32[]{:S(2)}) copy-start(bf16[1,768,1536]{2,1,0:T(8,128)(2,1)} %param.25) | copy-start | bytes 7077892
  15.5 37.9 %slice-start = ((s8[4718592]{0:T(1024)(128)(4,1)}), s8[4194304]{0:T(1024)(128)(4,1)S(1)}, s32[]{:S(2)}) async-start(s8[4718592]{0:T(1024)(128)(4,1)} %bitcast.168), calls=%async_computation.12 | async-start | bytes 8388608
  47.7 1.1 copy-start.12
  48.9 4.5 slice-start.1
  53.4 3.8 copy-start.23
  57.2 5.4 %copy-start.16 = (s32[256,1]{0,1:T(1,128)S(1)}, s32[256,1]{0,1:T(1,128)}, u32[]{:S(2)}) copy-start(s32[256,1]{0,1:T(1,128)} %param.17) | copy-start | bytes 3076
  57.2 6.4 %copy-start.19 = (s32[256]{0:T(256)S(1)}, s32[256]{0:T(256)}, u32[]{:S(2)}) copy-start(s32[256]{0:T(256)} %param.19) | copy-start | bytes 3076
  57.2 28.5 %all-to-all-start.1 = ((bf16[16,32,1536]{2,1,0:T(8,128)(2,1)}), bf16[16,32,1536]{2,1,0:T(8,128)(2,1)}, u32[]{:S(2)}, u32[]{:S(2)}) async-start(bf16[16,32,1536]{2,1,0:T(8,128)(2,1)} %bitcast.155), calls=%async_computation.1 | async-start | bytes 3145728 | tf_op jit(solution)/shard_map/all_to_all | solution.py:72
  85.7 4.6 copy-start.2
  85.7 4.6 copy-start.18
  99.9 7.9 %copy-start.9 = (bf16[256,1536]{1,0:T(8,128)(2,1)S(1)}, bf16[256,1536]{1,0:T(8,128)(2,1)}, u32[]{:S(2)}) copy-start(bf16[256,1536]{1,0:T(8,128)(2,1)} %param.15) | copy-start | bytes 2359300
  99.9 7.9 %copy-start.17 = (f32[256,1]{0,1:T(1,128)S(1)}, f32[256,1]{0,1:T(1,128)}, u32[]{:S(2)}) copy-start(f32[256,1]{0,1:T(1,128)} %param.21) | copy-start | bytes 3076
  99.9 47.9 %all-to-all-start.2 = ((bf16[128,8,1536]{2,1,0:T(8,128)(2,1)}), bf16[128,8,1536]{2,1,0:T(8,128)(2,1)}, u32[]{:S(2)}, u32[]{:S(2)}) async-start(bf16[128,8,1536]{2,1,0:T(8,128)(2,1)} %bitcast.148), calls=%async_computation.2 | async-start | bytes 6291456 | tf_op jit(solution)/shard_map/all_to_all | solution.py:76
  151.0 46.0 %all-to-all-start.4 = ((bf16[128,8,1536]{2,1,0:T(8,128)(2,1)}), bf16[128,8,1536]{2,1,0:T(8,128)(2,1)}, u32[]{:S(2)}, u32[]{:S(2)}) async-start(bf16[128,8,1536]{2,1,0:T(8,128)(2,1)} %bitcast.147), calls=%async_computation.4 | async-start | bytes 6291456 | tf_op jit(solution)/shard_map/all_to_all | solution.py:76
  162.1 1.6 copy-start.21
  197.0 46.1 %all-to-all-start.3 = ((bf16[128,8,1536]{2,1,0:T(8,128)(2,1)}), bf16[128,8,1536]{2,1,0:T(8,128)(2,1)}, u32[]{:S(2)}, u32[]{:S(2)}) async-start(bf16[128,8,1536]{2,1,0:T(8,128)(2,1)} %fusion.11), calls=%async_computation.3 | async-start | bytes 6291456 | tf_op jit(solution)/shard_map/all_to_all | solution.py:76
  203.0 7.2 %copy-start.20 = (bf16[1,1536,768]{2,1,0:T(8,128)(2,1)S(1)}, bf16[1,1536,768]{2,1,0:T(8,128)(2,1)}, u32[]{:S(2)}) copy-start(bf16[1,1536,768]{2,1,0:T(8,128)(2,1)} %param.24) | copy-start | bytes 7077892
  209.0 1.2 copy-start.27
  243.2 46.1 %all-to-all-start.5 = ((bf16[128,8,1536]{2,1,0:T(8,128)(2,1)}), bf16[128,8,1536]{2,1,0:T(8,128)(2,1)}, u32[]{:S(2)}, u32[]{:S(2)}) async-start(bf16[128,8,1536]{2,1,0:T(8,128)(2,1)} %fusion.12), calls=%async_computation.5 | async-start | bytes 6291456 | tf_op jit(solution)/shard_map/all_to_all | solution.py:76
  249.1 210.1 %reduce-scatter.5.cloned.1.call-start = ((), (), s32[]{:S(2)}) async-start(), calls=%async_computation.11 | async-start | bytes 5308416 | tf_op jit(solution)/shard_map/reduce_scatter | solution.py:159
  293.7 1.3 copy-start.4
  295.0 0.9 copy-start.7
  295.0 1.4 copy-start.10
  295.0 1.6 copy-start.11
  299.5 30.3 %copy-start.5 = (bf16[256,1536]{1,0:T(8,128)(2,1)}, bf16[256,1536]{1,0:T(8,128)(2,1)S(1)}, u32[]{:S(2)}) copy-start(bf16[256,1536]{1,0:T(8,128)(2,1)S(1)} %get-tuple-element.13) | copy-start | bytes 2359300
  301.9 29.0 %copy-start.24 = (f32[512,1536]{1,0:T(8,128)S(1)}, f32[512,1536]{1,0:T(8,128)}, u32[]{:S(2)}) copy-start(f32[512,1536]{1,0:T(8,128)} %copy-done.23) | copy-start | bytes 9437188
  329.8 1.1 copy-start.14
  335.2 1.4 copy-start.15
  335.2 8.4 %copy-start.13 = (bf16[16,32,1536]{2,1,0:T(8,128)(2,1)S(1)}, bf16[16,32,1536]{2,1,0:T(8,128)(2,1)}, u32[]{:S(2)}) copy-start(bf16[16,32,1536]{2,1,0:T(8,128)(2,1)} %copy-done.12) | copy-start | bytes 4718596
  335.3 124.0 %reduce-scatter.3.cloned.1.call-start = ((), (), s32[]{:S(2)}) async-start(), calls=%async_computation.10 | async-start | bytes 5308416 | tf_op jit(solution)/shard_map/reduce_scatter | solution.py:156
  342.5 1.1 copy-start.25
  348.0 1.4 copy-start.26
  355.6 5.1 %copy-start.28 = (bf16[1024,768]{1,0:T(8,128)(2,1)S(1)}, bf16[1024,768]{1,0:T(8,128)(2,1)}, u32[]{:S(2)}) copy-start(bf16[1024,768]{1,0:T(8,128)(2,1)} %copy-done.27) | copy-start | bytes 4718596
  355.6 97.7 %all-to-all-start.7 = ((bf16[16,32,1536]{2,1,0:T(8,128)(2,1)}), bf16[16,32,1536]{2,1,0:T(8,128)(2,1)S(1)}, u32[]{:S(2)}, u32[]{:S(2)}) async-start(bf16[16,32,1536]{2,1,0:T(8,128)(2,1)} %bitcast.30), calls=%async_computation.7 | async-start | bytes 3145728 | tf_op jit(solution)/shard_map/all_to_all | solution.py:72
  360.7 6.1 %copy-start.22 = (f32[1024,768]{1,0:T(8,128)S(1)}, f32[1024,768]{1,0:T(8,128)}, u32[]{:S(2)}) copy-start(f32[1024,768]{1,0:T(8,128)} %copy-done.21) | copy-start | bytes 9437188
  453.3 2.2 copy-start.3
  454.6 0.9 copy-start.8
  455.5 1.1 copy-start.6
  455.9 3.3 copy-start.1
Sparse Core Ops, SparseCore 0:
  335.4 53.8 reduce-scatter.4
  392.3 56.8 reduce-scatter.2
where the time goes:
time: 475 us; the launch traced here: 466 us
  waiting for transfers between devices  235 us (49%)
  matrix products  60.2 us (13%)
  blocking collectives  60.1 us (13%)
  starting transfers between devices  36.4 us (8%)
  other arithmetic  31.7 us (7%)
  local copies, waits for them, and re-layouts  28 us (6%)
  between operations  14.8 us (3%)
    all_to_all x4, waiting for transfers between devices, wide_route(): lax.all_to_all(buffer, ('ex', 'ey'), split_axis=0, concat_axis=0, tiled=T...  133 us
    all_to_all x2, waiting for transfers between devices, first_return(): return lax.all_to_all(filled, 'ex', split_axis=0, concat_axis=0, tiled=True)  103 us
    all_to_all x2, blocking collectives, first_send(): return lax.all_to_all(filled, 'ex', split_axis=0, concat_axis=0, tiled=True)  60.1 us
    all_to_all x4, starting transfers between devices, wide_route(): lax.all_to_all(buffer, ('ex', 'ey'), split_axis=0, concat_axis=0, tiled=T...  25.5 us
    dot_general x4, matrix products, product_back(): lax.dot_general(left_side, right_side, (((1,), (1,)), ((), ())), preferre...  22 us
    dot_general x4, matrix products, product_rows(): lax.dot_general(left_side, right_side, (((0,), (0,)), ((), ())), preferre...  20.7 us
    dot_general x4, matrix products, product(): return jnp.dot(left_side, right_side, preferred_element_type=jnp.float32)  17.5 us
    scatter x4, other arithmetic, fill_slots(): filled = jnp.zeros((experts * capacity, values.shape[1]), values.dtype).a...  13.2 us
  transfers between devices with their start and end apart: 8, of which 6 were waited for; matrix products, arithmetic and copies ran while one was open for 13% of the time, Pallas kernels for 0%

commit v1 on v0

v1 whole, which is shorter than its diff:
```python
import jax
import jax.numpy as jnp
from jax import lax
from jax.experimental import pallas as pl
from jax.experimental.pallas import tpu as pltpu
from jax.sharding import Mesh
from jax.sharding import PartitionSpec as P

EPS = 1e-06
AXES = ("y_hi", "z", "core", "y_lo", "x")
EX = ("y_hi", "z", "core")
EY = ("y_lo", "x")
CHIPS = ("y_hi", "z", "y_lo", "x")
EXPERTS_ONE, CAP_ONE = 16, 32
EXPERTS_TWO, CAP_TWO = 64, 8
BF, F32 = jnp.bfloat16, jnp.float32
CHUNK = 256


def dot(left, right):
    return jnp.dot(left, right, preferred_element_type=F32)


def dot_nt(left, right):
    return lax.dot_general(left, right, (((1,), (1,)), ((), ())), preferred_element_type=F32)


def dot_tn(left, right):
    return lax.dot_general(left, right, (((0,), (0,)), ((), ())), preferred_element_type=F32)


def iota(shape, axis):
    return lax.broadcasted_iota(jnp.int32, shape, axis)


def slot_targets(route, keep, experts, cap, index_of):
    count = route.shape[1]
    chosen = iota((experts, count), 0) == route
    earlier = (iota((count, count), 0) < iota((count, count), 1)).astype(F32).astype(BF)
    before = dot(chosen.astype(F32).astype(BF), earlier)
    rank = jnp.sum(jnp.where(chosen, before, 0.0), axis=0, keepdims=True).astype(jnp.int32)
    return jnp.where(keep > 0, index_of(route) * cap + rank, -1)


def chip_of(expert):
    return (expert // 8) * 8 + (expert % 4) * 2 + (expert // 4) % 2


def column_of(row):
    count = row.shape[1]
    same = iota((count, count), 0) == iota((count, count), 1)
    return jnp.sum(jnp.where(same, row, jnp.zeros_like(row)), axis=1, keepdims=True)


def place_matrix(target, slots):
    return (iota((slots, target.shape[1]), 0) == target).astype(F32).astype(BF)


def collect_matrix(target, slots):
    column = column_of(target.astype(F32)).astype(jnp.int32)
    return (iota((target.shape[1], slots), 1) == column).astype(F32).astype(BF)


def fill(out_ref, target, rows):
    matrix = place_matrix(target, out_ref.shape[0])
    for start in range(0, out_ref.shape[1], CHUNK):
        part = slice(start, start + CHUNK)
        out_ref[:, part] = dot(matrix, rows[:, part]).astype(out_ref.dtype)


def inverse_rms(values):
    return lax.rsqrt(jnp.mean(values * values, axis=-1, keepdims=True) + EPS)


def rms_back(values, grad):
    inv = inverse_rms(values)
    normed = values * inv
    return inv * (grad - normed * jnp.mean(grad * normed, axis=-1, keepdims=True))


def first_kernel(tok, up, route1, keep1, route2, keep2, gate2, rows1, rows2, target1, target2):
    to_one = slot_targets(route1[...], keep1[...], EXPERTS_ONE, CAP_ONE, lambda e: e)
    to_two = slot_targets(route2[...], keep2[...], EXPERTS_TWO, CAP_TWO, chip_of)
    target1[...] = to_one
    target2[...] = to_two
    values = tok[...].astype(F32)
    fill(rows1, to_one, (values * inverse_rms(values)).astype(BF))
    fill(rows2, to_two, (column_of(gate2[...]) * up[...].astype(F32)).astype(BF))


def middle_kernel(tok, returned, target1, target2, gate1, middle, rows2):
    gathered = dot(collect_matrix(target1[...], returned.shape[0]), returned[...])
    mid = (tok[...].astype(F32) + column_of(gate1[...]) * gathered).astype(BF)
    middle[...] = mid
    values = mid.astype(F32)
    fill(rows2, target2[...], (values * inverse_rms(values)).astype(BF))


def turn_kernel(middle, up, returned, target1, target2, gate1, grad_middle, rows1):
    gathered = dot(collect_matrix(target2[...], returned.shape[0]), returned[...])
    grad = (up[...].astype(F32) + rms_back(middle[...].astype(F32), gathered)).astype(BF)
    grad_middle[...] = grad
    fill(rows1, target1[...], (column_of(gate1[...]) * grad.astype(F32)).astype(BF))


def result_kernel(middle, returned, target2, gate2, result):
    gathered = dot(collect_matrix(target2[...], returned.shape[0]), returned[...])
    result[...] = (middle[...].astype(F32) + column_of(gate2[...]) * gathered).astype(BF)


def last_kernel(tok, grad_middle, returned, target1, grad_tokens):
    gathered = dot(collect_matrix(target1[...], returned.shape[0]), returned[...])
    grad_tokens[...] = (
        grad_middle[...].astype(F32) + rms_back(tok[...].astype(F32), gathered)
    ).astype(BF)


def call(kernel, outs, *args):
    moved = sum(a.size * a.dtype.itemsize for a in args)
    return pl.pallas_call(
        kernel,
        out_shape=outs,
        compiler_params=pltpu.CompilerParams(vmem_limit_bytes=32 * 1024 * 1024),
        cost_estimate=pl.CostEstimate(
            flops=2 * 256 * 512 * 1536, bytes_accessed=2 * moved, transcendentals=0
        ),
    )(*args)


def shape(rows, columns, dtype=BF):
    return jax.ShapeDtypeStruct((rows, columns), dtype)


def exchange_one(rows):
    width = rows.shape[1]
    parts = rows.reshape(EXPERTS_ONE, CAP_ONE, width)
    return lax.all_to_all(parts, EX, split_axis=0, concat_axis=0, tiled=True).reshape(-1, width)


def exchange_two(rows):
    width = rows.shape[1]
    parts = rows.reshape(EXPERTS_TWO, CAP_TWO, width)
    return lax.all_to_all(parts, CHIPS, split_axis=0, concat_axis=0, tiled=True).reshape(-1, width)


def swap_pairs(values):
    size = 4
    pairs = []
    for x in range(size):
        if x % 2 == 0:
            pairs += [(x, x), (size + x, x + 1)]
        else:
            pairs += [(x, size + x - 1), (size + x, size + x)]
    return lax.ppermute(values, ("core", "x"), pairs)


def other_core(values):
    return lax.ppermute(values, "core", [(0, 1), (1, 0)])


def silu_slope(preact):
    sigmoid_value = jax.nn.sigmoid(preact)
    return sigmoid_value * (1.0 + preact * (1.0 - sigmoid_value))


def per_device(
    tokens,
    upstream,
    route_one,
    route_two,
    keep_one,
    keep_two,
    gate_one,
    gate_two,
    up_one,
    down_one,
    up_two,
    down_two,
):
    count, width = tokens.shape
    slots_one, slots_two = EXPERTS_ONE * CAP_ONE, EXPERTS_TWO * CAP_TWO
    route_one, route_two, keep_one, keep_two, gate_one, gate_two = (
        v.reshape(1, count) for v in (route_one, route_two, keep_one, keep_two, gate_one, gate_two)
    )
    up_mine = swap_pairs(up_two[0])
    down_mine = swap_pairs(down_two[0])
    up_other = other_core(up_mine)
    down_other = other_core(down_mine)

    filled_one, filled_grads, target_one, target_two = call(
        first_kernel,
        (
            shape(slots_one, width),
            shape(slots_two, width),
            shape(1, count, jnp.int32),
            shape(1, count, jnp.int32),
        ),
        tokens, upstream, route_one, keep_one, route_two, keep_two, gate_two,
    )
    rows_one = exchange_one(filled_one)
    pre_one = dot(rows_one, up_one[0])
    hidden_one = jax.nn.silu(pre_one).astype(BF)
    returned_one = exchange_one(dot(hidden_one, down_one[0]).astype(BF))
    grads_two = exchange_two(filled_grads)

    middle, filled_two = call(
        middle_kernel,
        (shape(count, width), shape(slots_two, width)),
        tokens, returned_one, target_one, target_two, gate_one,
    )
    rows_two = exchange_two(filled_two)
    pre_mine = dot(rows_two, up_mine)
    pre_other = dot(rows_two, up_other)
    inner_mine = (dot_nt(grads_two, down_mine) * silu_slope(pre_mine)).astype(BF)
    inner_other = (dot_nt(grads_two, down_other) * silu_slope(pre_other)).astype(BF)
    back_two = (dot_nt(inner_mine, up_mine) + dot_nt(inner_other, up_other)).astype(BF)
    returned_back = exchange_two(back_two)
    hidden_mine = jax.nn.silu(pre_mine).astype(BF)
    hidden_other = jax.nn.silu(pre_other).astype(BF)
    out_two = (dot(hidden_mine, down_mine) + dot(hidden_other, down_other)).astype(BF)
    returned_out = exchange_two(out_two)
    term_up_two = other_core(dot_tn(rows_two, inner_other).astype(BF))
    term_down_two = other_core(dot_tn(hidden_other, grads_two).astype(BF))
    grad_up_two = swap_pairs((dot_tn(rows_two, inner_mine) + term_up_two.astype(F32)).astype(BF))
    grad_down_two = swap_pairs(
        (dot_tn(hidden_mine, grads_two) + term_down_two.astype(F32)).astype(BF)
    )

    grad_middle, filled_back = call(
        turn_kernel,
        (shape(count, width), shape(slots_one, width)),
        middle, upstream, returned_back, target_one, target_two, gate_one,
    )
    result = call(
        result_kernel, shape(count, width), middle, returned_out, target_two, gate_two
    )
    grads_one = exchange_one(filled_back)
    inner_one = (dot_nt(grads_one, down_one[0]) * silu_slope(pre_one)).astype(BF)
    back_one = dot_nt(inner_one, up_one[0]).astype(BF)
    returned_last = exchange_one(back_one)
    share_down = lax.psum_scatter(
        dot_tn(hidden_one, grads_one).astype(BF), EY, scatter_dimension=0, tiled=True
    )
    share_up = lax.psum_scatter(
        dot_tn(rows_one, inner_one).astype(BF), EY, scatter_dimension=0, tiled=True
    )
    grad_tokens = call(
        last_kernel, shape(count, width), tokens, grad_middle, returned_last, target_one
    )
    return (
        result,
        grad_tokens,
        share_up[None],
        share_down[None],
        grad_up_two[None],
        grad_down_two[None],
    )


def solution(mesh):
    fine = Mesh(mesh.devices.reshape(2, 4, 2, 2, 4), AXES)
    rows = P(AXES, None)
    weights = P(AXES, None, None)
    return jax.shard_map(
        per_device,
        mesh=fine,
        in_specs=(
            rows, rows, rows, rows, P(AXES), P(AXES), rows, rows,
            P(EX, None, None), P(EX, None, None), weights, weights,
        ),
        out_specs=(rows, rows, P(EX, EY, None), P(EX, EY, None), weights, weights),
        check_vma=False,
    )
```

time: 475 us -> 430 us (0.905)
  waiting for transfers between devices: 235 us -> 116 us
  blocking collectives: 60.1 us -> 142 us
  other arithmetic: 31.7 us -> 0.01 us
  starting transfers between devices: 36.4 us -> 48.6 us
  matrix products: 60.2 us -> 72.3 us
  Pallas kernels: 0 us -> 8.82 us
  local copies, waits for them, and re-layouts: 28 us -> 22 us
    all_to_all x6 -> x4, waiting for transfers between devices: 235 us -> 108 us  [the longest x2 70.7 us: exchange_one(): lax.all_to_all(parts, EX, split_axis=0, concat_axis=0, tiled=True)]
    all_to_all x2 -> x4, blocking collectives: 60.1 us -> 142 us  [the longest x2 81.6 us: exchange_two(): lax.all_to_all(parts, CHIPS, split_axis=0, concat_axis=0, tiled=True)]
    ppermute x0 -> x8, starting transfers between devices: none -> 13.6 us  [the longest x4 11.5 us: swap_pairs(): return lax.ppermute(values, ('core', 'x'), pairs)]
    scatter x4 -> x0, other arithmetic: 13.2 us -> none  [fill_slots(): filled = jnp.zeros((experts * capacity, values.shape[1]), values.dtype).a...]
    dot_general x12 -> x18, matrix products: 60.2 us -> 72.3 us  [the longest x6 25.7 us: dot_tn(): lax.dot_general(left, right, (((0,), (0,)), ((), ())), preferred_element_...]
    convert_element_type x6 -> x0, other arithmetic: 10.7 us -> none  [the longest x2 4.53 us: second_return(): (returned[:, 0].astype(jnp.float32) + returned[:, 1].astype(jnp.float32))...]
    unnamed x62 -> x78, local copies, waits for them, and re-layouts: 11.7 us -> 22 us
    gather x4 -> x0, local copies, waits for them, and re-layouts: 9.22 us -> none  [read_slots(): jnp.take(filled.reshape(-1, filled.shape[-1]), target, axis=0, mode='fill...]
  transfers between devices with their start and end apart: 8 -> 14, of which waited for: 6 -> 5; matrix products, arithmetic and copies ran while one was open for 13% -> 13% of each run, Pallas kernels for 0% -> 1%
where the time goes in v1:
time: 430 us; the launch traced here: 424 us
  blocking collectives  142 us (33%)
  waiting for transfers between devices  116 us (27%)
  matrix products  72.3 us (17%)
  starting transfers between devices  48.6 us (11%)
  local copies, waits for them, and re-layouts  22 us (5%)
  between operations  14.5 us (3%)
  Pallas kernels  8.82 us (2%)
    all_to_all x2, blocking collectives, exchange_two(): lax.all_to_all(parts, CHIPS, split_axis=0, concat_axis=0, tiled=True)  81.6 us
    all_to_all x2, waiting for transfers between devices, exchange_one(): lax.all_to_all(parts, EX, split_axis=0, concat_axis=0, tiled=True)  70.7 us
    all_to_all x2, blocking collectives, exchange_one(): lax.all_to_all(parts, EX, split_axis=0, concat_axis=0, tiled=True)  60.2 us
    all_to_all x2, waiting for transfers between devices, exchange_two(): lax.all_to_all(parts, CHIPS, split_axis=0, concat_axis=0, tiled=True)  37.6 us
    dot_general x6, matrix products, dot_tn(): lax.dot_general(left, right, (((0,), (0,)), ((), ())), preferred_element_...  25.7 us
    all_to_all x2, starting transfers between devices, exchange_one(): lax.all_to_all(parts, EX, split_axis=0, concat_axis=0, tiled=True)  25.3 us
    dot_general x6, matrix products, dot_nt(): lax.dot_general(left, right, (((1,), (1,)), ((), ())), preferred_element_...  25.1 us
    unnamed x78, local copies, waits for them, and re-layouts  22 us
  transfers between devices with their start and end apart: 14, of which 5 were waited for; matrix products, arithmetic and copies ran while one was open for 13% of the time, Pallas kernels for 1%

profile of v1, /device:TPU:1, one launch (start us, length us, event | category | flops | bytes accessed | tf_op | source)
XLA Modules:
  0.0 424.0 jit_solution(3816195819800613034)
XLA Ops:
  12.8 2.4 shard_map.163
  15.2 32.0 %all_to_all.40 = bf16[16,32,1536]{2,1,0:T(8,128)(2,1)S(1)} all-to-all(bf16[16,32,1536]{2,1,0:T(8,128)(2,1)S(1)} %bitcast.94), channel_id=1, replica_groups=mesh['y_hi'=2,'z'=4,'core'=2,'y_lo'=2,'x'=4] {'y_hi','z','core'}, dimensions={0} | all-to-all | bytes 3145728 | tf_op jit(solution)/shard_map/all_to_all | solution.py:137
  47.3 1.2 copy-done.20
  48.5 2.6 fusion.6
  51.1 3.8 fusion.16
  54.9 4.8 %all-to-all-start.1 = ((bf16[16,32,1536]{2,1,0:T(8,128)(2,1)}), bf16[16,32,1536]{2,1,0:T(8,128)(2,1)S(1)}, u32[]{:S(2)}, u32[]{:S(2)}) async-start(bf16[16,32,1536]{2,1,0:T(8,128)(2,1)} %bitcast.110), calls=%async_computation.1 | async-start | bytes 3145728 | tf_op jit(solution)/shard_map/all_to_all | solution.py:137
  59.7 3.2 collective-permute-start
  62.9 2.3 collective-permute-start.1
  65.3 17.4 %all-to-all-done.1 = bf16[16,32,1536]{2,1,0:T(8,128)(2,1)S(1)} async-done(((bf16[16,32,1536]{2,1,0:T(8,128)(2,1)}), bf16[16,32,1536]{2,1,0:T(8,128)(2,1)S(1)}, u32[]{:S(2)}, u32[]{:S(2)}) %all-to-all-start.1) | async-done | bytes 1572896 | tf_op jit(solution)/shard_map/all_to_all | solution.py:137
  82.6 1.4 shard_map.164
  84.0 54.7 %all_to_all.41 = bf16[64,8,1536]{2,1,0:T(8,128)(2,1)} all-to-all(bf16[64,8,1536]{2,1,0:T(8,128)(2,1)S(1)} %bitcast.95), channel_id=1, replica_groups=mesh['y_hi'=2,'z'=4,'core'=2,'y_lo'=2,'x'=4] {'y_hi','z','y_lo','x'}, dimensions={0} | all-to-all | bytes 3145728 | tf_op jit(solution)/shard_map/all_to_all | solution.py:143
  138.7 4.7 %all-to-all-start.4 = ((bf16[64,8,1536]{2,1,0:T(8,128)(2,1)}), bf16[64,8,1536]{2,1,0:T(8,128)(2,1)S(1)}, u32[]{:S(2)}, u32[]{:S(2)}) async-start(bf16[64,8,1536]{2,1,0:T(8,128)(2,1)} %bitcast.18), calls=%async_computation.4 | async-start | bytes 3145728 | tf_op jit(solution)/shard_map/all_to_all | solution.py:143
  144.4 4.7 %fusion.38 = f32[512,768]{1,0:T(8,128)} fusion(bf16[1536,768]{1,0:T(8,128)(2,1)} %collective-permute-done, bf16[64,8,1536]{2,1,0:T(8,128)(2,1)} %all_to_all.41), kind=kOutput, calls=%fused_computation.38 | convolution fusion | flops 1207959552 | bytes 5505024 | tf_op jit(solution)/shard_map/dot_general | solution.py:21
  149.1 18.0 %all-to-all-done.4 = bf16[64,8,1536]{2,1,0:T(8,128)(2,1)S(1)} async-done(((bf16[64,8,1536]{2,1,0:T(8,128)(2,1)}), bf16[64,8,1536]{2,1,0:T(8,128)(2,1)S(1)}, u32[]{:S(2)}, u32[]{:S(2)}) %all-to-all-start.4) | async-done | bytes 1572896 | tf_op jit(solution)/shard_map/all_to_all | solution.py:143
  167.1 4.3 %multiply_convert_fusion.2 = bf16[512,768]{1,0:T(8,128)(2,1)S(1)} fusion(f32[512,768]{1,0:T(8,128)} %fusion.38, bf16[768,1536]{1,0:T(8,128)(2,1)} %collective-permute-done.1, bf16[64,8,1536]{2,1,0:T(8,128)(2,1)S(1)} %all-to-all-done.4), kind=kOutput, calls=%fused_computation.41 | convolution fusion | flops 1211498496 | bytes 6291456 | tf_op jit(solution)/shard_map/dot_general | solution.py:25
  171.4 3.4 fusion.47
  174.8 3.0 fusion.36
  179.0 3.3 multiply_convert_fusion.1
  182.4 3.4 fusion.22
  185.8 27.0 %all_to_all.42 = bf16[64,8,1536]{2,1,0:T(8,128)(2,1)S(1)} all-to-all(bf16[64,8,1536]{2,1,0:T(8,128)(2,1)S(1)} %fusion.22), channel_id=1, replica_groups=mesh['y_hi'=2,'z'=4,'core'=2,'y_lo'=2,'x'=4] {'y_hi','z','y_lo','x'}, dimensions={0} | all-to-all | bytes 3145728 | tf_op jit(solution)/shard_map/all_to_all | solution.py:143
  212.8 1.6 shard_map.166
  214.4 28.1 %all_to_all.43 = bf16[16,32,1536]{2,1,0:T(8,128)(2,1)S(1)} all-to-all(bf16[16,32,1536]{2,1,0:T(8,128)(2,1)S(1)} %bitcast.96), channel_id=1, replica_groups=mesh['y_hi'=2,'z'=4,'core'=2,'y_lo'=2,'x'=4] {'y_hi','z','core'}, dimensions={0} | all-to-all | bytes 3145728 | tf_op jit(solution)/shard_map/all_to_all | solution.py:137
  242.5 1.1 copy-done.22
  243.7 4.4 %convolution_convert_fusion = bf16[1536,1536]{1,0:T(8,128)(2,1)} fusion(bf16[512,1536]{1,0:T(8,128)(2,1)S(1)} %bitcast.108, f32[512,1536]{1,0:T(8,128)S(1)} %copy-done.31), kind=kOutput, calls=%fused_computation | convolution fusion | flops 2422210560 | bytes 9437184 | tf_op jit(solution)/shard_map/dot_general | solution.py:29
  248.4 7.0 %fusion.19 = bf16[512,1536]{1,0:T(8,128)(2,1)S(1)} fusion(f32[512,1536]{1,0:T(8,128)} %copy-done.30, bf16[512,1536]{1,0:T(8,128)(2,1)} %bitcast.109, bf16[1,1536,1536]{2,1,0:T(8,128)(2,1)} %param.21), kind=kOutput, calls=%fused_computation.23 | convolution fusion | flops 2422996992 | bytes 11010048 | tf_op jit(solution)/shard_map/dot_general | solution.py:25
  255.4 1.2 copy-done.32
  256.6 4.4 %convolution_convert_fusion.1 = bf16[1536,1536]{1,0:T(8,128)(2,1)} fusion(bf16[512,1536]{1,0:T(8,128)(2,1)S(1)} %bitcast.106, bf16[512,1536]{1,0:T(8,128)(2,1)S(1)} %fusion.19), kind=kOutput, calls=%fused_computation.1 | convolution fusion | flops 2418278400 | bytes 7864320 | tf_op jit(solution)/shard_map/dot_general | solution.py:29
  261.0 1.4 copy-done.19
  262.4 4.1 convolution_convert_fusion.3
  267.7 2.9 convolution_convert_fusion.2
  270.6 3.1 fusion.46
  273.7 4.3 %fusion.23 = bf16[64,8,1536]{2,1,0:T(8,128)(2,1)} fusion(f32[512,1536]{1,0:T(8,128)S(1)} %fusion.46, bf16[768,1536]{1,0:T(8,128)(2,1)} %collective-permute-done.3, f32[512,768]{1,0:T(8,128)S(1)} %copy-done.28), kind=kOutput, calls=%fused_computation.25 | convolution fusion | flops 1211498496 | bytes 8650752 | tf_op jit(solution)/shard_map/dot_general | solution.py:21
  277.9 4.7 %all-to-all-start.3 = ((bf16[64,8,1536]{2,1,0:T(8,128)(2,1)}), bf16[64,8,1536]{2,1,0:T(8,128)(2,1)S(1)}, u32[]{:S(2)}, u32[]{:S(2)}) async-start(bf16[64,8,1536]{2,1,0:T(8,128)(2,1)} %fusion.23), calls=%async_computation.3 | async-start | bytes 3145728 | tf_op jit(solution)/shard_map/all_to_all | solution.py:143
  282.6 5.4 %add_convert_fusion.1 = bf16[1536,768]{1,0:T(8,128)(2,1)} fusion(bf16[1536,768]{1,0:T(8,128)(2,1)} %collective-permute-done.4, bf16[512,768]{1,0:T(8,128)(2,1)} %copy-done.29, bf16[64,8,1536]{2,1,0:T(8,128)(2,1)} %all_to_all.41), kind=kOutput, calls=%fused_computation.11 | convolution fusion | flops 1211498496 | bytes 7077888 | tf_op jit(solution)/shard_map/dot_general | solution.py:29
  288.1 3.9 collective-permute-start.5
  292.0 4.5 %add_convert_fusion = bf16[768,1536]{1,0:T(8,128)(2,1)} fusion(bf16[768,1536]{1,0:T(8,128)(2,1)} %collective-permute-done.6, bf16[64,8,1536]{2,1,0:T(8,128)(2,1)S(1)} %copy-done.17, f32[512,768]{1,0:T(8,128)S(1)} %copy-done.26), kind=kOutput, calls=%fused_computation.10 | convolution fusion | flops 1213464576 | bytes 7864320 | tf_op jit(solution)/shard_map/dot_general | solution.py:29
  296.5 2.0 collective-permute-start.7
  298.6 3.8 fusion.13
  302.4 19.5 %all-to-all-done.3 = bf16[64,8,1536]{2,1,0:T(8,128)(2,1)S(1)} async-done(((bf16[64,8,1536]{2,1,0:T(8,128)(2,1)}), bf16[64,8,1536]{2,1,0:T(8,128)(2,1)S(1)}, u32[]{:S(2)}, u32[]{:S(2)}) %all-to-all-start.3) | async-done | bytes 1572896 | tf_op jit(solution)/shard_map/all_to_all | solution.py:143
  321.9 1.2 copy-done.2
  323.1 20.6 %all-to-all-start.7 = ((bf16[16,32,1536]{2,1,0:T(8,128)(2,1)}), bf16[16,32,1536]{2,1,0:T(8,128)(2,1)S(1)}, u32[]{:S(2)}, u32[]{:S(2)}) async-start(bf16[16,32,1536]{2,1,0:T(8,128)(2,1)} %bitcast.107), calls=%async_computation.7 | async-start | bytes 3145728 | tf_op jit(solution)/shard_map/all_to_all | solution.py:137
  343.7 1.4 copy-done.3
  345.1 1.5 shard_map.165
  346.6 53.3 %all-to-all-done.7 = bf16[16,32,1536]{2,1,0:T(8,128)(2,1)S(1)} async-done(((bf16[16,32,1536]{2,1,0:T(8,128)(2,1)}), bf16[16,32,1536]{2,1,0:T(8,128)(2,1)S(1)}, u32[]{:S(2)}, u32[]{:S(2)}) %all-to-all-start.7) | async-done | bytes 1572896 | tf_op jit(solution)/shard_map/all_to_all | solution.py:137
  401.0 1.9 shard_map.167
  402.9 7.8 %collective-permute-done.7 = bf16[768,1536]{1,0:T(8,128)(2,1)} collective-permute-done((bf16[768,1536]{1,0:T(8,128)(2,1)}, bf16[768,1536]{1,0:T(8,128)(2,1)}, u32[]{:S(2)}, u32[]{:S(2)}) %collective-permute-start.7) | collective-permute-done | bytes 2359328 | tf_op jit(solution)/shard_map/ppermute | solution.py:154
  410.7 3.2 copy.20
  414.0 3.2 copy.21
  (89 shorter events, 10.5 us)
Async XLA Ops:
  7.2 1.1 copy-start
  8.3 1.1 copy-start.4
  10.8 0.7 copy-start.12
  12.8 35.6 %copy-start.23 = (bf16[1,1536,1536]{2,1,0:T(8,128)(2,1)S(1)}, bf16[1,1536,1536]{2,1,0:T(8,128)(2,1)}, u32[]{:S(2)}) copy-start(bf16[1,1536,1536]{2,1,0:T(8,128)(2,1)} %param.20) | copy-start | bytes 14155780
  15.2 35.9 %slice-start = ((s8[4718592]{0:T(1024)(128)(4,1)}), s8[4194304]{0:T(1024)(128)(4,1)S(1)}, s32[]{:S(2)}) async-start(s8[4718592]{0:T(1024)(128)(4,1)} %bitcast.111), calls=%async_computation.12 | async-start | bytes 8388608
  47.3 1.2 copy-start.20
  48.5 2.6 slice-start.1
  51.1 3.8 copy-start.30
  54.9 27.7 %copy-start.1 = (bf16[256,1536]{1,0:T(8,128)(2,1)S(1)}, bf16[256,1536]{1,0:T(8,128)(2,1)}, u32[]{:S(2)}) copy-start(bf16[256,1536]{1,0:T(8,128)(2,1)} %tok.5) | copy-start | bytes 2359300
  54.9 27.7 %copy-start.8 = (f32[256,1]{0,1:T(1,128)S(1)}, f32[256,1]{0,1:T(1,128)}, u32[]{:S(2)}) copy-start(f32[256,1]{0,1:T(1,128)} %param.18) | copy-start | bytes 3076
  54.9 27.7 %all-to-all-start.1 = ((bf16[16,32,1536]{2,1,0:T(8,128)(2,1)}), bf16[16,32,1536]{2,1,0:T(8,128)(2,1)S(1)}, u32[]{:S(2)}, u32[]{:S(2)}) async-start(bf16[16,32,1536]{2,1,0:T(8,128)(2,1)} %bitcast.110), calls=%async_computation.1 | async-start | bytes 3145728 | tf_op jit(solution)/shard_map/all_to_all | solution.py:137
  59.7 83.7 %collective-permute-start = (bf16[1536,768]{1,0:T(8,128)(2,1)}, bf16[1536,768]{1,0:T(8,128)(2,1)}, u32[]{:S(2)}, u32[]{:S(2)}) collective-permute-start(bf16[1536,768]{1,0:T(8,128)(2,1)} %bitcast.115), channel_id=1, source_target_pairs={{0,0},{8,1},{1,8},{9,9},{2,2},{10,3},{3,10},{11,11},{4,4},{12,5},{... | collective-permute-start | bytes 7077896 | tf_op jit(solution)/shard_map/ppermute | solution.py:154
  62.9 81.2 %collective-permute-start.1 = (bf16[768,1536]{1,0:T(8,128)(2,1)}, bf16[768,1536]{1,0:T(8,128)(2,1)}, u32[]{:S(2)}, u32[]{:S(2)}) collective-permute-start(bf16[768,1536]{1,0:T(8,128)(2,1)} %bitcast.116), channel_id=1, source_target_pairs={{0,0},{8,1},{1,8},{9,9},{2,2},{10,3},{3,10},{11,11},{4,4},{12,5},{... | collective-permute-start | bytes 7077896 | tf_op jit(solution)/shard_map/ppermute | solution.py:154
  138.7 28.4 %all-to-all-start.4 = ((bf16[64,8,1536]{2,1,0:T(8,128)(2,1)}), bf16[64,8,1536]{2,1,0:T(8,128)(2,1)S(1)}, u32[]{:S(2)}, u32[]{:S(2)}) async-start(bf16[64,8,1536]{2,1,0:T(8,128)(2,1)} %bitcast.18), calls=%async_computation.4 | async-start | bytes 3145728 | tf_op jit(solution)/shard_map/all_to_all | solution.py:143
  143.4 267.4 %reduce-scatter.5.cloned.1.call-start = ((), (), s32[]{:S(2)}) async-start(), calls=%async_computation.11 | async-start | bytes 5308416 | tf_op jit(solution)/shard_map/reduce_scatter | solution.py:241
  143.4 31.4 %collective-permute-start.2 = (bf16[1536,768]{1,0:T(8,128)(2,1)}, bf16[1536,768]{1,0:T(8,128)(2,1)}, u32[]{:S(2)}, u32[]{:S(2)}) collective-permute-start(bf16[1536,768]{1,0:T(8,128)(2,1)} %collective-permute-done), channel_id=1, source_target_pairs={{0,8},{8,0},{1,9},{9,1},{2,10},{10,2},{3,11},{11,3},{4,12},{12,4},... | collective-permute-start | bytes 7077896 | tf_op jit(solution)/shard_map/ppermute | solution.py:158
  144.1 33.8 %collective-permute-start.3 = (bf16[768,1536]{1,0:T(8,128)(2,1)}, bf16[768,1536]{1,0:T(8,128)(2,1)}, u32[]{:S(2)}, u32[]{:S(2)}) collective-permute-start(bf16[768,1536]{1,0:T(8,128)(2,1)} %collective-permute-done.1), channel_id=1, source_target_pairs={{0,8},{8,0},{1,9},{9,1},{2,10},{10,2},{3,11},{11,3},{4,12},{12,4},... | collective-permute-start | bytes 7077896 | tf_op jit(solution)/shard_map/ppermute | solution.py:158
  167.1 10.8 %copy-start.15 = (bf16[64,8,1536]{2,1,0:T(8,128)(2,1)}, bf16[64,8,1536]{2,1,0:T(8,128)(2,1)S(1)}, u32[]{:S(2)}) copy-start(bf16[64,8,1536]{2,1,0:T(8,128)(2,1)S(1)} %all-to-all-done.4) | copy-start | bytes 4718596
  171.4 3.4 copy-start.29
  171.4 3.4 copy-start.18
  177.9 1.1 copy-start.27
  182.4 3.4 copy-start.24
  185.8 27.0 %copy-start.5 = (bf16[256,1536]{1,0:T(8,128)(2,1)S(1)}, bf16[256,1536]{1,0:T(8,128)(2,1)}, u32[]{:S(2)}) copy-start(bf16[256,1536]{1,0:T(8,128)(2,1)} %up.3) | copy-start | bytes 2359300
  214.4 28.2 %copy-start.6 = (bf16[256,1536]{1,0:T(8,128)(2,1)}, bf16[256,1536]{1,0:T(8,128)(2,1)S(1)}, u32[]{:S(2)}) copy-start(bf16[256,1536]{1,0:T(8,128)(2,1)S(1)} %get-tuple-element.20.grad_middle) | copy-start | bytes 2359300
  214.4 29.3 %copy-start.31 = (f32[512,1536]{1,0:T(8,128)S(1)}, f32[512,1536]{1,0:T(8,128)}, u32[]{:S(2)}) copy-start(f32[512,1536]{1,0:T(8,128)} %copy-done.30) | copy-start | bytes 9437188
  242.5 1.1 copy-start.22
  248.1 8.5 %copy-start.21 = (bf16[16,32,1536]{2,1,0:T(8,128)(2,1)S(1)}, bf16[16,32,1536]{2,1,0:T(8,128)(2,1)}, u32[]{:S(2)}) copy-start(bf16[16,32,1536]{2,1,0:T(8,128)(2,1)} %copy-done.20) | copy-start | bytes 4718596
  248.1 162.6 %reduce-scatter.3.cloned.1.call-start = ((), (), s32[]{:S(2)}) async-start(), calls=%async_computation.10 | async-start | bytes 5308416 | tf_op jit(solution)/shard_map/reduce_scatter | solution.py:244
  255.4 1.2 copy-start.32
  261.0 1.4 copy-start.19
  262.4 5.3 %copy-start.16 = (bf16[64,8,1536]{2,1,0:T(8,128)(2,1)S(1)}, bf16[64,8,1536]{2,1,0:T(8,128)(2,1)}, u32[]{:S(2)}) copy-start(bf16[64,8,1536]{2,1,0:T(8,128)(2,1)} %copy-done.15) | copy-start | bytes 4718596
  262.4 5.3 %copy-start.28 = (f32[512,768]{1,0:T(8,128)S(1)}, f32[512,768]{1,0:T(8,128)}, u32[]{:S(2)}) copy-start(f32[512,768]{1,0:T(8,128)} %copy-done.27) | copy-start | bytes 4718596
  266.6 4.0 copy-start.25
  266.6 16.1 %collective-permute-start.4 = (bf16[1536,768]{1,0:T(8,128)(2,1)}, bf16[1536,768]{1,0:T(8,128)(2,1)}, u32[]{:S(2)}, u32[]{:S(2)}) collective-permute-start(bf16[1536,768]{1,0:T(8,128)(2,1)} %convolution_convert_fusion.3), channel_id=1, source_target_pairs={{0,8},{8,0},{1,9},{9,1},{2,10},{10,2},{3,11},{11,3},{4,12},{12,4},... | collective-permute-start | bytes 7077896 | tf_op jit(solution)/shard_map/ppermute | solution.py:158
  270.6 21.4 %collective-permute-start.6 = (bf16[768,1536]{1,0:T(8,128)(2,1)}, bf16[768,1536]{1,0:T(8,128)(2,1)}, u32[]{:S(2)}, u32[]{:S(2)}) collective-permute-start(bf16[768,1536]{1,0:T(8,128)(2,1)} %convolution_convert_fusion.2), channel_id=1, source_target_pairs={{0,8},{8,0},{1,9},{9,1},{2,10},{10,2},{3,11},{11,3},{4,12},{12,4},... | collective-permute-start | bytes 7077896 | tf_op jit(solution)/shard_map/ppermute | solution.py:158
  277.9 44.0 %all-to-all-start.3 = ((bf16[64,8,1536]{2,1,0:T(8,128)(2,1)}), bf16[64,8,1536]{2,1,0:T(8,128)(2,1)S(1)}, u32[]{:S(2)}, u32[]{:S(2)}) async-start(bf16[64,8,1536]{2,1,0:T(8,128)(2,1)} %fusion.23), calls=%async_computation.3 | async-start | bytes 3145728 | tf_op jit(solution)/shard_map/all_to_all | solution.py:143
  282.6 9.4 %copy-start.17 = (bf16[64,8,1536]{2,1,0:T(8,128)(2,1)S(1)}, bf16[64,8,1536]{2,1,0:T(8,128)(2,1)}, u32[]{:S(2)}) copy-start(bf16[64,8,1536]{2,1,0:T(8,128)(2,1)} %copy-done.15) | copy-start | bytes 4718596
  282.6 9.4 %copy-start.26 = (f32[512,768]{1,0:T(8,128)S(1)}, f32[512,768]{1,0:T(8,128)}, u32[]{:S(2)}) copy-start(f32[512,768]{1,0:T(8,128)} %fusion.38) | copy-start | bytes 4718596
  282.6 16.0 %slice-start.2 = ((s8[4718592]{0:T(1024)(128)(4,1)}), s8[4194304]{0:T(1024)(128)(4,1)S(1)}, s32[]{:S(2)}) async-start(s8[4718592]{0:T(1024)(128)(4,1)} %bitcast.113), calls=%async_computation.14 | async-start | bytes 8388608
  288.0 10.5 %slice-start.3 = ((s8[4718592]{0:T(1024)(128)(4,1)}), s8[524288]{0:T(1024)(128)(4,1)S(1)}, s32[]{:S(2)}) async-start(s8[4718592]{0:T(1024)(128)(4,1)} %bitcast.113), calls=%async_computation.15 | async-start | bytes 1048576
  288.1 10.6 %copy-start.33 = (bf16[512,1536]{1,0:T(8,128)(2,1)S(1)}, bf16[512,1536]{1,0:T(8,128)(2,1)}, u32[]{:S(2)}) copy-start(bf16[512,1536]{1,0:T(8,128)(2,1)} %copy-done.32) | copy-start | bytes 4718596
  288.1 114.9 %collective-permute-start.5 = (bf16[1536,768]{1,0:T(8,128)(2,1)}, bf16[1536,768]{1,0:T(8,128)(2,1)}, u32[]{:S(2)}, u32[]{:S(2)}) collective-permute-start(bf16[1536,768]{1,0:T(8,128)(2,1)} %add_convert_fusion.1), channel_id=1, source_target_pairs={{0,0},{8,1},{1,8},{9,9},{2,2},{10,3},{3,10},{11,11},{4,4},{12,5},{... | collective-permute-start | bytes 7077896 | tf_op jit(solution)/shard_map/ppermute | solution.py:154
  296.5 114.2 %collective-permute-start.7 = (bf16[768,1536]{1,0:T(8,128)(2,1)}, bf16[768,1536]{1,0:T(8,128)(2,1)}, u32[]{:S(2)}, u32[]{:S(2)}) collective-permute-start(bf16[768,1536]{1,0:T(8,128)(2,1)} %add_convert_fusion), channel_id=1, source_target_pairs={{0,0},{8,1},{1,8},{9,9},{2,2},{10,3},{3,10},{11,11},{4,4},{12,5},{... | collective-permute-start | bytes 7077896 | tf_op jit(solution)/shard_map/ppermute | solution.py:154
  321.9 1.2 copy-start.2
  323.1 20.6 %copy-start.10 = (f32[256,1]{0,1:T(1,128)S(1)}, f32[256,1]{0,1:T(1,128)}, u32[]{:S(2)}) copy-start(f32[256,1]{0,1:T(1,128)} %param.19) | copy-start | bytes 3076
  323.1 76.8 %all-to-all-start.7 = ((bf16[16,32,1536]{2,1,0:T(8,128)(2,1)}), bf16[16,32,1536]{2,1,0:T(8,128)(2,1)S(1)}, u32[]{:S(2)}, u32[]{:S(2)}) async-start(bf16[16,32,1536]{2,1,0:T(8,128)(2,1)} %bitcast.107), calls=%async_computation.7 | async-start | bytes 3145728 | tf_op jit(solution)/shard_map/all_to_all | solution.py:137
  343.7 1.4 copy-start.3
  399.9 1.1 copy-start.7
  (4 other events, 2.7 us)
Sparse Core Ops, SparseCore 0:
  248.2 71.5 reduce-scatter.4
  322.8 77.2 reduce-scatter.2
